TPU v7x, 256 devices: a whole 4x4x8 slice. The times are simulated.
256 devices in a mesh: seq: 32 (over y, z), blk: 8 (over x, core).
Axes of the slice: x: 4, y: 4, z: 8, core: 2. Of those that a mesh axis runs over, the one named last changes fastest.
Arguments:
- teacher_query: bfloat16 [8, 1024, 4096], P('blk', 'seq'), may hold values from -6 to 6
- teacher_key: bfloat16 [8, 1024, 4096], P('blk', 'seq'), may hold values from -6 to 6
- teacher_value: bfloat16 [8, 1024, 4096], P('blk', 'seq'), may hold values from -6 to 6
- student_query: bfloat16 [8, 1024, 4096], P('blk', 'seq'), may hold values from -6 to 6
- student_key: bfloat16 [8, 1024, 4096], P('blk', 'seq'), may hold values from -6 to 6
- student_value: bfloat16 [8, 1024, 4096], P('blk', 'seq'), may hold values from -6 to 6
- frame_index: int32 [8, 1024], P('blk', 'seq'), may hold values from 0 to 6, as said below
Outputs:
- query_grad: bfloat16 [8, 1024, 4096], P('blk', 'seq')
- key_grad: bfloat16 [8, 1024, 4096], P('blk', 'seq')
- value_grad: bfloat16 [8, 1024, 4096], P('blk', 'seq')
Inputs may be any that keep to these rules, and one draw needn't show every extreme that they name: `frame_index`: read row after row, frame numbers never fall; every frame 0 to 6 holds at least (6144) // 6 - 6144 // 24 tokens and at most 2048, and one frame holds exactly 2048.
All inputs are finite; a program needn't handle non-finite values.
Results may differ from a plain program's by a relative error of at most 0.028.
Values may be sent and summed in bfloat16 or wider, within the bound.
No kernel may reach another device: no remote copies, remote signals or barrier semaphores. Data moves between devices by JAX's collectives and lax.ppermute only.
A program may use at most 64 MiB of HBM per device.

v0:
```python
import math

import jax
import jax.numpy as jnp
from jax import lax
from jax.sharding import PartitionSpec as P

DH = 128


loss_scale = 64.0
masked_score = -1e30


def split_heads(flat_rows):
    return flat_rows.reshape(flat_rows.shape[:-1] + (flat_rows.shape[-1] // DH, DH))


def join_heads(stacked):
    return stacked.reshape(stacked.shape[0], -1)


def over_blocks(state, pieces, update):
    row_count = pieces[0].shape[0]
    block_len = math.gcd(row_count, 512)
    block_count = row_count // block_len
    stacked = tuple(
        (member.reshape((block_count, block_len) + member.shape[1:]) for member in pieces)
    )

    def over_advance(current, inputs):
        blocks, block_index = inputs
        return (update(current, blocks, block_index * block_len), None)

    result, ignored = lax.scan(
        over_advance, state, (stacked, jnp.arange(block_count, dtype=jnp.int32))
    )
    return result


def softmax_step(state, queries, key_rows, value_rows, visible):
    maxima, totals, summed = state
    scores = jnp.einsum(
        "qhd,khd->hqk", queries, split_heads(key_rows), preferred_element_type=jnp.float32
    ) * DH ** (-0.5)
    if visible is not None:
        scores = jnp.where(visible[None], scores, masked_score)
    new_max = jnp.maximum(maxima, jnp.max(scores, axis=-1))
    weights = jnp.exp(scores - new_max[..., None])
    if visible is not None:
        weights = jnp.where(visible[None], weights, 0.0)
    rescale = jnp.exp(maxima - new_max)
    totals = totals * rescale + jnp.sum(weights, axis=-1)
    summed = summed * rescale[..., None] + jnp.einsum(
        "hqk,khd->hqd",
        weights.astype(jnp.bfloat16),
        split_heads(value_rows),
        preferred_element_type=jnp.float32,
    )
    return (new_max, totals, summed)


def tile_gradients(queries, out_grads, maxima, totals, deltas, key_split, value_split, visible):
    scores = jnp.einsum(
        "qhd,khd->hqk", queries, key_split, preferred_element_type=jnp.float32
    ) * DH ** (-0.5)
    attention = jnp.where(
        visible[None], jnp.exp(scores - maxima[..., None]) / totals[..., None], 0.0
    )
    attention_grad = jnp.einsum(
        "hqd,khd->hqk", out_grads, value_split, preferred_element_type=jnp.float32
    )
    score_grad = (attention * (attention_grad - deltas[..., None]) * DH ** (-0.5)).astype(
        jnp.bfloat16
    )
    return (attention, score_grad)


def per_device(
    teacher_query,
    teacher_key,
    teacher_value,
    student_query,
    student_key,
    student_value,
    frame_index,
):
    teacher_rows = (
        lax.all_to_all(teacher_query[0], "seq", split_axis=1, concat_axis=0, tiled=True),
        lax.all_to_all(teacher_key[0], "seq", split_axis=1, concat_axis=0, tiled=True),
        lax.all_to_all(teacher_value[0], "seq", split_axis=1, concat_axis=0, tiled=True),
    )
    student_rows = (
        lax.all_to_all(student_query[0], "seq", split_axis=1, concat_axis=0, tiled=True),
        lax.all_to_all(student_key[0], "seq", split_axis=1, concat_axis=0, tiled=True),
        lax.all_to_all(student_value[0], "seq", split_axis=1, concat_axis=0, tiled=True),
    )
    group_frames = lax.all_gather(frame_index[0], "seq", axis=0, tiled=True)
    all_frames = lax.all_gather(group_frames, "blk", axis=0, tiled=True)
    group_rows = group_frames.shape[0]
    head_count = teacher_rows[0].shape[1] // DH
    latest = jnp.max(group_frames)
    teacher_queries = split_heads(teacher_rows[0])
    student_queries = split_heads(student_rows[0])
    blank = (
        jnp.full((head_count, group_rows), masked_score, jnp.float32),
        jnp.zeros((head_count, group_rows), jnp.float32),
        jnp.zeros((head_count, group_rows, DH), jnp.float32),
    )

    def teacher_update(state, blocks, key_offset):
        return softmax_step(state, teacher_queries, blocks[0], blocks[1], None)

    def student_update(state, blocks, key_offset):
        key_frames = lax.dynamic_slice_in_dim(all_frames, key_offset, blocks[0].shape[0])

        def student_compute():
            visible = key_frames[None, :] <= group_frames[:, None]
            return softmax_step(state, student_queries, blocks[0], blocks[1], visible)

        return lax.cond(jnp.min(key_frames) <= latest, student_compute, lambda: state)

    teacher_state = over_blocks(
        blank,
        (
            lax.all_gather(teacher_rows[1], "blk", axis=0, tiled=True),
            lax.all_gather(teacher_rows[2], "blk", axis=0, tiled=True),
        ),
        teacher_update,
    )
    student_state = over_blocks(
        blank,
        (
            lax.all_gather(student_rows[1], "blk", axis=0, tiled=True),
            lax.all_gather(student_rows[2], "blk", axis=0, tiled=True),
        ),
        student_update,
    )
    target = (teacher_state[2] / teacher_state[1][..., None]).astype(jnp.bfloat16)
    maxima, totals, summed = student_state
    output = summed / totals[..., None]
    out_grads = (loss_scale * (output - target.astype(jnp.float32))).astype(jnp.bfloat16)
    deltas = jnp.sum(out_grads.astype(jnp.float32) * output, axis=-1)
    grad_zeros = jnp.zeros((group_rows, head_count, DH), jnp.float32)
    key_all, value_all = (
        lax.all_gather(student_rows[1], "blk", axis=0, tiled=True),
        lax.all_gather(student_rows[2], "blk", axis=0, tiled=True),
    )
    all_rows = key_all.shape[0]
    block_len = math.gcd(all_rows, 512)
    block_count = all_rows // block_len

    def body_advance(state, inputs):
        key_block, value_block, block_index = inputs
        key_frames = lax.dynamic_slice_in_dim(all_frames, block_index * block_len, block_len)
        key_split = split_heads(key_block)
        value_split = split_heads(value_block)

        def body_compute():
            visible = key_frames[None, :] <= group_frames[:, None]
            attention, score_grad = tile_gradients(
                student_queries, out_grads, maxima, totals, deltas, key_split, value_split, visible
            )
            query_part = jnp.einsum(
                "hqk,khd->qhd", score_grad, key_split, preferred_element_type=jnp.float32
            )
            key_part = jnp.einsum(
                "hqk,qhd->khd", score_grad, student_queries, preferred_element_type=jnp.float32
            )
            value_part = jnp.einsum(
                "hqk,hqd->khd",
                attention.astype(jnp.bfloat16),
                out_grads,
                preferred_element_type=jnp.float32,
            )
            return (state + query_part, key_part, value_part)

        def skipped():
            empty_part = jnp.zeros((block_len, head_count, DH), jnp.float32)
            return (state, empty_part, empty_part)

        new_state, key_part, value_part = lax.cond(
            jnp.min(key_frames) <= latest, body_compute, skipped
        )
        return (new_state, (key_part, value_part))

    query_grad, (key_parts, value_parts) = lax.scan(
        body_advance,
        grad_zeros,
        (
            key_all.reshape(block_count, block_len, -1),
            value_all.reshape(block_count, block_len, -1),
            jnp.arange(block_count, dtype=jnp.int32),
        ),
    )
    key_grad, value_grad = (
        lax.psum_scatter(
            key_parts.reshape(all_rows, -1).astype(jnp.bfloat16),
            "blk",
            scatter_dimension=0,
            tiled=True,
        ).astype(jnp.float32),
        lax.psum_scatter(
            value_parts.reshape(all_rows, -1).astype(jnp.bfloat16),
            "blk",
            scatter_dimension=0,
            tiled=True,
        ).astype(jnp.float32),
    )
    query_rows = join_heads(query_grad).astype(jnp.bfloat16)
    key_rows = key_grad.astype(jnp.bfloat16)
    value_rows = value_grad.astype(jnp.bfloat16)
    results = (
        lax.all_to_all(query_rows, "seq", split_axis=0, concat_axis=1, tiled=True),
        lax.all_to_all(key_rows, "seq", split_axis=0, concat_axis=1, tiled=True),
        lax.all_to_all(value_rows, "seq", split_axis=0, concat_axis=1, tiled=True),
    )
    return (results[0][None], results[1][None], results[2][None])


def solution(mesh):
    return jax.shard_map(
        per_device,
        mesh=mesh,
        in_specs=(
            P("blk", "seq", None),
            P("blk", "seq", None),
            P("blk", "seq", None),
            P("blk", "seq", None),
            P("blk", "seq", None),
            P("blk", "seq", None),
            P("blk", "seq"),
        ),
        out_specs=(P("blk", "seq", None), P("blk", "seq", None), P("blk", "seq", None)),
        check_vma=False,
    )
```

profile of v0, /device:TPU:32, one launch (start us, length us, event | category | flops | bytes accessed | tf_op | source)
XLA Modules:
  0.0 546.1 jit_solution(8777121229396564442)
XLA Ops:
  8.4 23.6 %all_to_all.153 = bf16[32,32,128]{2,0,1:T(8,128)(2,1)} all-to-all(bf16[32,32,128]{2,0,1:T(8,128)(2,1)S(1)} %copy.38), channel_id=1, replica_groups=mesh['seq'=32,'blk'=8] {'seq'}, dimensions={1} | all-to-all | bytes 524288 | tf_op jit(solution)/shard_map/all_to_all | solution.py:95
  33.1 15.9 %all_to_all.154 = bf16[32,32,128]{2,0,1:T(8,128)(2,1)} all-to-all(bf16[32,32,128]{2,0,1:T(8,128)(2,1)S(1)} %copy.40), channel_id=1, replica_groups=mesh['seq'=32,'blk'=8] {'seq'}, dimensions={1} | all-to-all | bytes 524288 | tf_op jit(solution)/shard_map/all_to_all | solution.py:96
  49.3 15.7 %all_to_all.155 = bf16[32,32,128]{2,0,1:T(8,128)(2,1)} all-to-all(bf16[32,32,128]{2,0,1:T(8,128)(2,1)S(1)} %copy.41), channel_id=1, replica_groups=mesh['seq'=32,'blk'=8] {'seq'}, dimensions={1} | all-to-all | bytes 524288 | tf_op jit(solution)/shard_map/all_to_all | solution.py:90
  65.2 15.3 %all_to_all.156 = bf16[32,32,128]{2,0,1:T(8,128)(2,1)} all-to-all(bf16[32,32,128]{2,0,1:T(8,128)(2,1)S(1)} %copy.43), channel_id=1, replica_groups=mesh['seq'=32,'blk'=8] {'seq'}, dimensions={1} | all-to-all | bytes 524288 | tf_op jit(solution)/shard_map/all_to_all | solution.py:91
  81.4 4.4 all-to-all-start.1
  88.1 20.0 %all-reduce = s32[1024]{0:T(1024)S(1)} all-reduce(s32[1024]{0:T(1024)S(1)} %bitcast_dynamic-update-slice_fusion), channel_id=2, replica_groups=mesh['seq'=32,'blk'=8] {'seq'}, use_global_device_ids=true, to_apply=%add | all-reduce | flops 1024 | bytes 8192 | tf_op jit(solution)/shard_map/all_gather | solution.py:98
  108.7 13.2 %all-gather.1 = s32[1,8192]{1,0:T(1,128)S(1)} all-gather(s32[1,1024]{1,0:T(1,128)S(1)} %bitcast.211), channel_id=3, replica_groups=mesh['seq'=32,'blk'=8] {'blk'}, dimensions={1}, use_global_device_ids=true | all-gather | bytes 36864 | tf_op jit(solution)/shard_map/all_gather | solution.py:99
  121.9 5.4 all-to-all-start.4
  127.5 66.7 %while.46 = (s32[]{:T(128)}, f32[1,1024]{1,0:T(1,128)S(1)}, f32[1,1024]{1,0:T(1,128)S(1)}, f32[1,1024,128]{2,1,0:T(8,128)S(1)}, s32[16]{0:T(128)S(1)}, /*index=5...) while((s32[]{:T(128)}, f32[1,1024]{1,0:T(1,128)S(1)}, ...), condition=%wide.region_7.8_spmd, body=%wide.region_1.7_spmd.sunk | while | flops 277088768 | bytes 7953765 | solution.py:35
  130.9 3.9 conditional.4
  133.0 1.8 fusion.3
  138.2 3.9 conditional.4
  140.3 1.8 fusion.3
  145.6 3.9 conditional.4
  147.6 1.8 fusion.3
  194.2 53.6 %while.48 = (s32[]{:T(128)}, f32[1,1024]{1,0:T(1,128)S(1)}, f32[1,1024]{1,0:T(1,128)S(1)}, f32[1,1024,128]{2,1,0:T(8,128)S(1)}, bf16[16,512,128]{2,1,0:T(8,128)(...) while((s32[]{:T(128)}, f32[1,1024]{1,0:T(1,128)S(1)}, ...), condition=%wide.region_11.12_spmd.clone, body=%wide.region_8.11_spmd.clone.sunk | while | flops 273028096 | bytes 7929977 | solution.py:35
  196.0 1.5 fusion.75
  199.4 1.5 fusion.75
  202.7 1.5 fusion.75
  248.4 79.5 %while.47 = (s32[]{:T(128)}, f32[1024,1,128]{0,2,1:T(8,128)S(1)}, bf16[16,512,1,128]{3,1,2,0:T(8,128)(2,1)}, bf16[16,512,1,128]{3,1,2,0:T(8,128)(2,1)}, s32[16]{...) while((s32[]{:T(128)}, f32[1024,1,128]{0,2,1:T(8,128)S(1)}, ...), condition=%wide.region_17.18_spmd, body=%wide.region_13.17_spmd.sunk | while | flops 676463104 | bytes 12738933 | solution.py:187
  251.7 5.1 conditional.5
  251.7 1.6 bitcast_select_fusion
  260.7 5.1 conditional.5
  260.7 1.6 bitcast_select_fusion
  269.8 5.1 conditional.5
  269.8 1.6 bitcast_select_fusion
  328.7 20.6 %all_to_all.157 = bf16[32,32,128]{2,1,0:T(8,128)(2,1)S(1)} all-to-all(bf16[32,32,128]{2,1,0:T(8,128)(2,1)S(1)} %bitcast.192), channel_id=1, replica_groups=mesh['seq'=32,'blk'=8] {'seq'}, dimensions={0} | all-to-all | bytes 524288 | tf_op jit(solution)/shard_map/all_to_all | solution.py:214
  349.3 130.4 %reduce-scatter.3.cloned.1.call-done = bf16[1024,128]{1,0:T(8,128)(2,1)} async-done(((bf16[8192,128]{1,0:T(8,128)(2,1)}), bf16[1024,128]{1,0:T(8,128)(2,1)}) %reduce-scatter.3.cloned.1.call-update) | async-done | bytes 262160 | tf_op jit(solution)/shard_map/reduce_scatter | solution.py:197
  479.7 10.1 %all-to-all-start.7 = ((bf16[32,32,128]{2,1,0:T(8,128)(2,1)}), bf16[32,32,128]{2,1,0:T(8,128)(2,1)S(1)}, u32[]{:S(2)}, u32[]{:S(2)}) async-start(bf16[32,32,128]{2,1,0:T(8,128)(2,1)} %bitcast.219), calls=%async_computation.8 | async-start | bytes 524288 | tf_op jit(solution)/shard_map/all_to_all | solution.py:215
  489.8 27.5 %reduce-scatter.5.cloned.1.call-done = bf16[1024,128]{1,0:T(8,128)(2,1)} async-done(((bf16[8192,128]{1,0:T(8,128)(2,1)}), bf16[1024,128]{1,0:T(8,128)(2,1)}) %reduce-scatter.5.cloned.1.call-update) | async-done | bytes 262160 | tf_op jit(solution)/shard_map/reduce_scatter | solution.py:203
  517.3 10.0 %all-to-all-start.8 = ((bf16[32,32,128]{2,1,0:T(8,128)(2,1)}), bf16[32,32,128]{2,1,0:T(8,128)(2,1)S(1)}, u32[]{:S(2)}, u32[]{:S(2)}) async-start(bf16[32,32,128]{2,1,0:T(8,128)(2,1)} %bitcast.218), calls=%async_computation.10 | async-start | bytes 524288 | tf_op jit(solution)/shard_map/all_to_all | solution.py:216
  529.2 9.2 %all-to-all-done.8 = bf16[32,32,128]{2,1,0:T(8,128)(2,1)S(1)} async-done(((bf16[32,32,128]{2,1,0:T(8,128)(2,1)}), bf16[32,32,128]{2,1,0:T(8,128)(2,1)S(1)}, u32[]{:S(2)}, u32[]{:S(2)}) %all-to-all-start.8) | async-done | bytes 262176 | tf_op jit(solution)/shard_map/all_to_all | solution.py:216
  (318 shorter events, 131.5 us)
Async XLA Ops:
  7.2 41.9 %copy-start = (bf16[1,32,4096]{2,1,0:T(8,128)(2,1)S(1)}, bf16[1,32,4096]{2,1,0:T(8,128)(2,1)}, u32[]{:S(2)}) copy-start(bf16[1,32,4096]{2,1,0:T(8,128)(2,1)} %param.18) | copy-start | bytes 786436
  7.2 120.2 %all-gather.7.cloned.1.call-start = ((), (), s32[]{:S(2)}) async-start(), calls=%async_computation.11 | async-start | bytes 2359296 | tf_op jit(solution)/shard_map/all_gather | solution.py:146
  31.9 33.1 %copy-start.1 = (bf16[1,32,4096]{2,1,0:T(8,128)(2,1)S(1)}, bf16[1,32,4096]{2,1,0:T(8,128)(2,1)}, u32[]{:S(2)}) copy-start(bf16[1,32,4096]{2,1,0:T(8,128)(2,1)} %param.19) | copy-start | bytes 786436
  31.9 95.5 %all-gather.9.cloned.1.call-start = ((), (), s32[]{:S(2)}) async-start(), calls=%async_computation.12 | async-start | bytes 2359296 | tf_op jit(solution)/shard_map/all_gather | solution.py:147
  49.0 31.6 %copy-start.2 = (bf16[1,32,4096]{2,1,0:T(8,128)(2,1)S(1)}, bf16[1,32,4096]{2,1,0:T(8,128)(2,1)}, u32[]{:S(2)}) copy-start(bf16[1,32,4096]{2,1,0:T(8,128)(2,1)} %param.20) | copy-start | bytes 786436
  49.0 145.2 %all-gather.11.cloned.1.call-start = ((), (), s32[]{:S(2)}) async-start(), calls=%async_computation.13 | async-start | bytes 2359296 | tf_op jit(solution)/shard_map/all_gather | solution.py:126
  49.2 36.7 %copy-start.3 = (bf16[1,32,4096]{2,1,0:T(8,128)(2,1)S(1)}, bf16[1,32,4096]{2,1,0:T(8,128)(2,1)}, u32[]{:S(2)}) copy-start(bf16[1,32,4096]{2,1,0:T(8,128)(2,1)} %param.17) | copy-start | bytes 786436
  65.0 129.3 %all-gather.13.cloned.1.call-start = ((), (), s32[]{:S(2)}) async-start(), calls=%async_computation.14 | async-start | bytes 2359296 | tf_op jit(solution)/shard_map/all_gather | solution.py:127
  65.1 21.7 %copy-start.5 = (u32[256]{0:T(256)S(1)}, u32[256]{0:T(256)}, u32[]{:S(2)}) copy-start(u32[256]{0:T(256)} %constant.110) | copy-start | bytes 3076
  65.1 22.9 %copy-start.4 = (s32[1,32]{1,0:T(1,128)S(1)}, s32[1,32]{1,0:T(1,128)}, u32[]{:S(2)}) copy-start(s32[1,32]{1,0:T(1,128)} %param.23) | copy-start | bytes 388
  81.4 40.5 %all-to-all-start.1 = ((bf16[32,32,128]{2,0,1:T(8,128)(2,1)}), bf16[32,32,128]{2,0,1:T(8,128)(2,1)S(1)}, u32[]{:S(2)}, u32[]{:S(2)}) async-start(bf16[32,32,128]{2,0,1:T(8,128)(2,1)} %copy.39), calls=%async_computation.1 | async-start | bytes 524288 | tf_op jit(solution)/shard_map/all_to_all | solution.py:94
  121.9 72.3 %all-to-all-start.4 = ((bf16[32,32,128]{2,0,1:T(8,128)(2,1)}), bf16[32,32,128]{2,0,1:T(8,128)(2,1)S(1)}, u32[]{:S(2)}, u32[]{:S(2)}) async-start(bf16[32,32,128]{2,0,1:T(8,128)(2,1)} %copy.42), calls=%async_computation.4 | async-start | bytes 524288 | tf_op jit(solution)/shard_map/all_to_all | solution.py:89
  127.3 352.4 %reduce-scatter.3.cloned.1.call-start = ((), (), s32[]{:S(2)}) async-start(), calls=%async_computation.15 | async-start | bytes 2359296 | tf_op jit(solution)/shard_map/reduce_scatter | solution.py:197
  327.9 189.4 %reduce-scatter.5.cloned.1.call-start = ((), (), s32[]{:S(2)}) async-start(), calls=%async_computation.16 | async-start | bytes 2359296 | tf_op jit(solution)/shard_map/reduce_scatter | solution.py:203
  479.7 37.6 %all-to-all-start.7 = ((bf16[32,32,128]{2,1,0:T(8,128)(2,1)}), bf16[32,32,128]{2,1,0:T(8,128)(2,1)S(1)}, u32[]{:S(2)}, u32[]{:S(2)}) async-start(bf16[32,32,128]{2,1,0:T(8,128)(2,1)} %bitcast.219), calls=%async_computation.8 | async-start | bytes 524288 | tf_op jit(solution)/shard_map/all_to_all | solution.py:215
  517.3 21.1 %all-to-all-start.8 = ((bf16[32,32,128]{2,1,0:T(8,128)(2,1)}), bf16[32,32,128]{2,1,0:T(8,128)(2,1)S(1)}, u32[]{:S(2)}, u32[]{:S(2)}) async-start(bf16[32,32,128]{2,1,0:T(8,128)(2,1)} %bitcast.218), calls=%async_computation.10 | async-start | bytes 524288 | tf_op jit(solution)/shard_map/all_to_all | solution.py:216
Sparse Core Ops, SparseCore 0:
  32.1 23.4 all-gather.6
  57.5 28.0 all-gather.8
  87.4 28.0 all-gather.10
  117.2 28.0 all-gather.12
  328.0 151.5 reduce-scatter.2
  482.1 35.1 reduce-scatter.4
where the time goes:
time: 550 us; the launch traced here: 546 us
  waiting for transfers between devices  168 us (31%)
  blocking collectives  124 us (23%)
  matrix products  71 us (13%)
  loops' own time  64.8 us (12%)
  local copies, waits for them, and re-layouts  39.9 us (7%)
  other arithmetic  33.2 us (6%)
  starting transfers between devices  30.2 us (5%)
  between operations  15.1 us (3%)
    reduce_scatter x1, waiting for transfers between devices, per_device(): lax.psum_scatter(key_parts.reshape(all_rows, -1).astype(jnp.bfloat16), 'b...  130 us
    another operation x2, loops' own time, over_blocks(): lax.scan(over_advance, state, (stacked, jnp.arange(block_count, dtype=jnp...  32.9 us
    another operation x1, loops' own time, per_device(): lax.scan(body_advance, grad_zeros, (key_all.reshape(block_count, block_le...  31 us
    dot_general x19, matrix products, softmax_step(): jnp.einsum('hqk,khd->hqd', weights.astype(jnp.bfloat16), split_heads(valu...  30.1 us
    reduce_scatter x1, waiting for transfers between devices, per_device(): lax.psum_scatter(value_parts.reshape(all_rows, -1).astype(jnp.bfloat16),...  27.5 us
    dot_general x19, matrix products, softmax_step(): jnp.einsum('qhd,khd->hqk', queries, split_heads(key_rows), preferred_elem...  25.8 us
    all_to_all x1, blocking collectives, per_device(): lax.all_to_all(student_key[0], 'seq', split_axis=1, concat_axis=0, tiled=...  23.6 us
    all_to_all x1, blocking collectives, per_device(): lax.all_to_all(query_rows, 'seq', split_axis=0, concat_axis=1, tiled=True)  20.6 us
  transfers between devices with their start and end apart: 10, of which 3 were waited for; matrix products, arithmetic and copies ran while one was open for 7% of the time, Pallas kernels for 0%

commit v1 on v0

v1 whole, which is shorter than its diff:
```python
import functools

import jax
import jax.numpy as jnp
from jax import lax
from jax.experimental import pallas as pl
from jax.experimental.pallas import tpu as pltpu
from jax.sharding import PartitionSpec as P

DH = 128
HEADS = 32
SHARD = 32
ROWS = 1024
HALF = 512
TOKENS = 8192
EXTRA = 16
scale = DH ** -0.5
scale_log2 = scale * 1.4426950408889634
loss_scale = 64.0
hidden_bias = -131072.0
AXES = ("blk", "seq")
SETS = [[(j if s < 16 else 7 - j) * 32 + s for s in range(32)] for j in range(8)]
f32 = jnp.float32
bf16 = jnp.bfloat16
VMEM = pl.BlockSpec(memory_space=pltpu.VMEM)
SMEM = pl.BlockSpec(memory_space=pltpu.SMEM)
ANY = pl.BlockSpec(memory_space=pl.ANY)


def params():
    return pltpu.CompilerParams(vmem_limit_bytes=60 * 2**20)


def dot(a, b):
    return jnp.dot(a, b, preferred_element_type=f32)


def pack_queries_kernel(first_ref, second_ref, counts_ref, out_ref):
    for h in range(HEADS):
        cols = slice(h * DH, (h + 1) * DH)
        out_ref[h, :SHARD, :DH] = first_ref[:, cols]
        out_ref[h, :SHARD, DH:] = second_ref[:, cols]
        out_ref[h, SHARD:, :] = counts_ref[...]


def pack_queries(first, second, counts):
    return pl.pallas_call(
        pack_queries_kernel,
        out_shape=jax.ShapeDtypeStruct((HEADS, SHARD + EXTRA, 2 * DH), bf16),
        in_specs=[VMEM] * 3,
        out_specs=VMEM,
        compiler_params=params(),
    )(first, second, counts)


def pack_four_kernel(a_ref, b_ref, c_ref, d_ref, out_ref):
    for h in range(HEADS):
        cols = slice(h * DH, (h + 1) * DH)
        out_ref[h, :SHARD, :DH] = a_ref[:, cols]
        out_ref[h, :SHARD, DH:] = b_ref[:, cols]
        out_ref[h, SHARD:, :DH] = c_ref[:, cols]
        out_ref[h, SHARD:, DH:] = d_ref[:, cols]


def pack_four(a, b, c, d):
    return pl.pallas_call(
        pack_four_kernel,
        out_shape=jax.ShapeDtypeStruct((HEADS, 2 * SHARD, 2 * DH), bf16),
        in_specs=[VMEM] * 4,
        out_specs=VMEM,
        compiler_params=params(),
    )(a, b, c, d)


def unpack_one_kernel(in_ref, out_ref):
    for h in range(HEADS):
        out_ref[:, h * DH:(h + 1) * DH] = in_ref[h]


def unpack_one(rows):
    return pl.pallas_call(
        unpack_one_kernel,
        out_shape=jax.ShapeDtypeStruct((SHARD, HEADS * DH), bf16),
        in_specs=[VMEM],
        out_specs=VMEM,
        compiler_params=params(),
    )(rows)


def unpack_two_kernel(in_ref, first_ref, second_ref):
    for h in range(HEADS):
        cols = slice(h * DH, (h + 1) * DH)
        first_ref[:, cols] = in_ref[h, :, :DH]
        second_ref[:, cols] = in_ref[h, :, DH:]


def unpack_two(rows):
    return pl.pallas_call(
        unpack_two_kernel,
        out_shape=[jax.ShapeDtypeStruct((SHARD, HEADS * DH), bf16)] * 2,
        in_specs=[VMEM],
        out_specs=[VMEM] * 2,
        compiler_params=params(),
    )(rows)


def fold(op, x):
    return op(x.reshape(-1, 8, x.shape[-1]), axis=0)


def online_step(scores, values_t, cols, max_ref, sum_ref, out_ref):
    before = max_ref[0:1, cols]
    highest = jnp.max(fold(jnp.max, scores), axis=0, keepdims=True) * scale_log2
    now = jnp.maximum(before, highest)
    shrink = jnp.exp2(before - now)
    weights = jnp.exp2(scores * scale_log2 - now)
    rounded = weights.astype(bf16)
    block_sum = jnp.sum(fold(jnp.sum, weights), axis=0, keepdims=True)
    sum_ref[0:1, cols] = sum_ref[0:1, cols] * shrink + block_sum
    out_ref[:, cols] = out_ref[:, cols] * shrink + dot(values_t, rounded)
    max_ref[0:1, cols] = now
    return rounded, now


def clear(max_ref, sum_ref, out_ref):
    max_ref[...] = jnp.full(max_ref.shape, -1e30, f32)
    sum_ref[...] = jnp.zeros(sum_ref.shape, f32)
    out_ref[...] = jnp.zeros(out_ref.shape, f32)


def load_pieces(pieces, held, sems):
    copies = [
        pltpu.make_async_copy(piece, held.at[pl.ds(i * ROWS, ROWS)], sems.at[i])
        for i, piece in enumerate(pieces)
    ]
    for copy in copies:
        copy.start()
    return copies


def take_queries(q_ref, meta_ref, cols):
    parts = []
    for h in range(2):
        at = pl.ds(meta_ref[10 + h], SHARD // 2)
        parts.append(q_ref[at, :SHARD, cols].reshape(HALF, DH))
    return jnp.concatenate(parts, axis=0)


def rows_of(i):
    return pl.ds(pl.multiple_of(i * ROWS, ROWS), ROWS)


def teacher_kernel(meta_ref, q_ref, *rest):
    pieces = rest[:8]
    target_ref, held, max_ref, sum_ref, out_ref, sems = rest[8:]
    copies = load_pieces(pieces, held, sems)
    clear(max_ref, sum_ref, out_ref)
    queries_t = take_queries(q_ref, meta_ref, slice(0, DH)).T
    for copy in copies:
        copy.wait()

    def step(i, _):
        rows = rows_of(i)
        scores = dot(held[rows, :DH], queries_t)
        online_step(scores, held[rows, DH:].T, slice(0, ROWS), max_ref, sum_ref, out_ref)
        return 0

    lax.fori_loop(0, 8, step, 0)
    target_ref[...] = (out_ref[...] / sum_ref[0:1, :]).astype(bf16)


def teacher(meta, queries, pieces):
    return pl.pallas_call(
        teacher_kernel,
        out_shape=jax.ShapeDtypeStruct((DH, ROWS), bf16),
        in_specs=[SMEM, VMEM] + [ANY] * 8,
        out_specs=VMEM,
        scratch_shapes=[
            pltpu.VMEM((TOKENS, 2 * DH), bf16),
            pltpu.VMEM((8, ROWS), f32),
            pltpu.VMEM((8, ROWS), f32),
            pltpu.VMEM((DH, ROWS), f32),
            pltpu.SemaphoreType.DMA((8,)),
        ],
        compiler_params=params(),
        cost_estimate=pl.CostEstimate(
            flops=16 * 10**9, bytes_accessed=6 * 2**20, transcendentals=ROWS * TOKENS
        ),
    )(meta, queries, *pieces)


def frames_of(tokens, meta_ref):
    frames = jnp.zeros(tokens.shape, jnp.int32)
    for f in range(6):
        frames = frames + (tokens >= meta_ref[f]).astype(jnp.int32)
    return frames


def groups_seen(meta_ref, last):
    seen = jnp.int32(TOKENS)
    for f in range(6, -1, -1):
        seen = jnp.where(last < meta_ref[f], meta_ref[f], seen)
    return (seen + (ROWS - 1)) // ROWS


def keys_with_frames(keys, group, meta_ref):
    column = lax.broadcasted_iota(jnp.int32, (ROWS, DH), 1)
    tokens = group * ROWS + lax.broadcasted_iota(jnp.int32, (ROWS, DH), 0)
    one_hot = (frames_of(tokens, meta_ref) == column).astype(f32).astype(bf16)
    return jnp.concatenate([keys, one_hot], axis=1)


def by_visibility(meta_ref, group, compute, skip=None):
    seen_early = groups_seen(meta_ref, meta_ref[8] + (HALF - 1))
    seen_late = groups_seen(meta_ref, meta_ref[9] + (HALF - 1))

    @pl.when(group < seen_early)
    def _():
        compute(0)

    @pl.when((group >= seen_early) & (group < seen_late))
    def _():
        compute(HALF)

    if skip is not None:

        @pl.when(group >= seen_late)
        def _():
            skip()


def student_kernel(meta_ref, q_ref, target_ref, *rest):
    pieces = rest[:8]
    dq_ref = rest[8]
    outs = rest[9:15]
    held, max_ref, sum_ref, out_ref, weights_ref, max_at, dqt, qt_ref, kv_grad, sems, out_sems = rest[15:]
    copies = load_pieces(pieces, held, sems)
    clear(max_ref, sum_ref, out_ref)
    dqt[...] = jnp.zeros(dqt.shape, f32)
    queries = take_queries(q_ref, meta_ref, slice(DH, 2 * DH))
    column = lax.broadcasted_iota(jnp.int32, (DH, ROWS), 1)
    row = lax.broadcasted_iota(jnp.int32, (DH, ROWS), 0)
    tokens = jnp.where(column < HALF, meta_ref[8] + column, meta_ref[9] + (column - HALF))
    bias = jnp.where((row > frames_of(tokens, meta_ref)) & (row < 7), hidden_bias, 0.0)
    qt_ref[:DH, :] = queries.T
    qt_ref[DH:, :] = bias.astype(bf16)
    for copy in copies:
        copy.wait()

    def forward(i, _):
        group = meta_ref[16 + i]

        def compute(first):
            rows, cols = rows_of(i), slice(first, ROWS)
            keys = keys_with_frames(held[rows, :DH], group, meta_ref)
            rounded, now = online_step(
                dot(keys, qt_ref[:, cols]), held[rows, DH:].T, cols, max_ref, sum_ref, out_ref
            )
            weights_ref[rows, cols] = rounded
            at = pl.ds(pl.multiple_of(i * 8, 8), 8)
            max_at[at, cols] = jnp.broadcast_to(now, (8, ROWS - first))

        by_visibility(meta_ref, group, compute)
        return 0

    lax.fori_loop(0, 8, forward, 0)

    inverse = 1.0 / sum_ref[0:1, :]
    output = out_ref[...] * inverse
    out_grad = (loss_scale * (output - target_ref[...].astype(f32))).astype(bf16).astype(f32)
    delta = jnp.sum(out_grad * output, axis=0, keepdims=True) * inverse
    grad_t = (out_grad * inverse).astype(bf16)
    delta_1 = delta.astype(bf16).astype(f32)
    delta_2 = (delta - delta_1).astype(bf16).astype(f32)
    delta_3 = delta - delta_1 - delta_2
    delta_rows = jnp.where(
        row == 0, -delta_1, jnp.where(row == 1, -delta_2, jnp.where(row == 2, -delta_3, 0.0))
    )
    grad_delta_t = jnp.concatenate([grad_t, delta_rows.astype(bf16)], axis=0)
    grad = grad_t.T
    key_column = lax.broadcasted_iota(jnp.int32, (ROWS, DH), 1)
    ones = jnp.where(key_column < 3, 1.0, 0.0).astype(bf16)

    def backward(i, _):
        group = meta_ref[16 + i]

        def compute(first):
            rows, cols = rows_of(i), slice(first, ROWS)
            values = jnp.concatenate([held[rows, DH:], ones], axis=1)
            centred = dot(values, grad_delta_t[:, cols])
            at = pl.ds(pl.multiple_of(i * 8, 8), 8)
            shrink = jnp.exp2(max_at[at, cols][0:1] - max_ref[0:1, cols])
            weights = weights_ref[rows, cols].astype(f32) * shrink
            score_grad = (weights * centred).astype(bf16)
            kv_grad[rows, DH:] = dot(weights.astype(bf16), grad[cols]).astype(bf16)
            kv_grad[rows, :DH] = (dot(score_grad, queries[cols]) * scale).astype(bf16)
            dqt[:, cols] += dot(held[rows, :DH].T, score_grad)

        def skip():
            kv_grad[rows_of(i), :] = jnp.zeros((ROWS, 2 * DH), bf16)

        by_visibility(meta_ref, group, compute, skip)
        return 0

    lax.fori_loop(0, 8, backward, 0)
    out_copies = [
        pltpu.make_async_copy(kv_grad.at[pl.ds(i * ROWS, ROWS)], out, out_sems.at[k])
        for k, (i, out) in enumerate(
            [(0, outs[0]), (1, outs[1]), (2, outs[2].at[0]), (4, outs[2].at[1])]
            + [(3, outs[3].at[0]), (5, outs[3].at[1]), (6, outs[4]), (7, outs[5])]
        )
    ]
    for copy in out_copies:
        copy.start()
    query_grad = (dqt[...] * scale).T.astype(bf16)
    for h in range(2):
        at = pl.ds(pl.multiple_of(meta_ref[10 + h] * SHARD, HALF), HALF)
        dq_ref[at, :] = query_grad[h * HALF:(h + 1) * HALF]
    for copy in out_copies:
        copy.wait()


def student(meta, queries, target, pieces):
    one = jax.ShapeDtypeStruct((ROWS, 2 * DH), bf16)
    two = jax.ShapeDtypeStruct((2, ROWS, 2 * DH), bf16)
    return pl.pallas_call(
        student_kernel,
        out_shape=[jax.ShapeDtypeStruct((ROWS, DH), bf16), one, one, two, two, one, one],
        in_specs=[SMEM, VMEM, VMEM] + [ANY] * 8,
        out_specs=[VMEM] + [ANY] * 6,
        scratch_shapes=[
            pltpu.VMEM((TOKENS, 2 * DH), bf16),
            pltpu.VMEM((8, ROWS), f32),
            pltpu.VMEM((8, ROWS), f32),
            pltpu.VMEM((DH, ROWS), f32),
            pltpu.VMEM((TOKENS, ROWS), bf16),
            pltpu.VMEM((64, ROWS), f32),
            pltpu.VMEM((DH, ROWS), f32),
            pltpu.VMEM((2 * DH, ROWS), bf16),
            pltpu.VMEM((TOKENS, 2 * DH), bf16),
            pltpu.SemaphoreType.DMA((8,)),
            pltpu.SemaphoreType.DMA((8,)),
        ],
        compiler_params=params(),
        cost_estimate=pl.CostEstimate(
            flops=26 * 10**9, bytes_accessed=10 * 2**20, transcendentals=ROWS * TOKENS
        ),
    )(meta, queries, target, *pieces)


def exchange(packed, sets):
    return lax.all_to_all(
        packed, AXES, split_axis=0, concat_axis=0, tiled=True, axis_index_groups=sets
    )


def exchange_groups(packed):
    return lax.all_to_all(packed, "seq", split_axis=0, concat_axis=0, tiled=True)


def chip_shift(x, by):
    return lax.ppermute(x, "blk", [(i, ((i // 2 + by) % 4) * 2 + i % 2) for i in range(8)])


def swap_cores(x):
    return lax.ppermute(x, "blk", [(i, i ^ 1) for i in range(8)])


def chip_blocks(own):
    return [own] + [chip_shift(own, by) for by in (3, 1, 2)]


def with_other_core(parts):
    return [x for part in parts for x in (part, swap_cores(part))]


def frame_ends(counted):
    counts = jnp.broadcast_to(jnp.sum(counted.astype(f32), axis=0)[:, None], (8, DH))
    counts = counts + swap_cores(counts)
    counts = counts + chip_shift(counts, 1)
    counts = counts + chip_shift(counts, 2)
    return counts[:, 0].astype(jnp.int32)


def per_device(
    teacher_query,
    teacher_key,
    teacher_value,
    student_query,
    student_key,
    student_value,
    frame_index,
):
    blk = lax.axis_index("blk")
    seq = lax.axis_index("seq")
    keys_values = exchange_groups(
        pack_four(teacher_key[0], teacher_value[0], student_key[0], student_value[0])
    )
    teacher_kv = keys_values[:, :SHARD].reshape(ROWS, 2 * DH)
    teacher_parts = chip_blocks(teacher_kv)
    teacher_pieces = with_other_core(teacher_parts)
    teacher_query, keys_values = lax.optimization_barrier((teacher_query, keys_values))
    student_kv = keys_values[:, SHARD:].reshape(ROWS, 2 * DH)
    student_kv, _ = lax.optimization_barrier((student_kv, teacher_parts[3]))
    frame_ids = jnp.arange(2 * DH, dtype=jnp.int32)
    counts = jnp.sum((frame_index[0][:, None] <= frame_ids[None, :]).astype(f32), axis=0)
    counts = jnp.broadcast_to(counts.astype(bf16), (EXTRA, 2 * DH))
    queries = exchange(pack_queries(teacher_query[0], student_query[0], counts), SETS)
    ends = frame_ends(queries[:, SHARD, :8])
    student_parts = chip_blocks(student_kv)

    chip, core = blk // 2, blk % 2
    own_set = jnp.where(seq < 16, blk, 7 - blk)
    low, high = own_set * ROWS, (7 - own_set) * ROWS + HALF
    groups = []
    for by in (0, 1, 3, 2):
        groups += [((chip + by) % 4) * 2 + core, ((chip + by) % 4) * 2 + 1 - core]
    halves = jnp.stack([jnp.minimum(low, high), jnp.maximum(low, high)])
    members = jnp.where(low < high, jnp.array([0, SHARD // 2]), jnp.array([SHARD // 2, 0]))
    place = [halves, members, jnp.zeros((4,), jnp.int32), jnp.stack(groups)]
    place = jnp.concatenate([jnp.zeros((8,), jnp.int32)] + place).astype(jnp.int32)
    meta = jnp.concatenate([ends, place[8:]])

    target = teacher(place, queries, teacher_pieces)
    student_parts, target = lax.optimization_barrier((student_parts, target))
    student_pieces = with_other_core(student_parts)
    query_grad, here_mine, here_other, near_mine, near_other, far_mine, far_other = student(
        meta, queries, target, student_pieces
    )
    far = far_mine.astype(f32) + swap_cores(far_other).astype(f32)
    far = far.astype(bf16)
    relayed = [chip_shift(far[:HALF], 1), chip_shift(far[HALF:], 3)]
    near = near_mine.astype(f32) + swap_cores(near_other).astype(f32)
    ahead = jnp.concatenate([near[0, :HALF] + relayed[0].astype(f32), near[0, HALF:]]).astype(bf16)
    behind = jnp.concatenate([near[1, :HALF], near[1, HALF:] + relayed[1].astype(f32)]).astype(bf16)
    received = [chip_shift(ahead, 1), chip_shift(behind, 3)]
    total = here_mine.astype(f32) + swap_cores(here_other).astype(f32)
    for part in received:
        total = total + part.astype(f32)
    query_out = unpack_one(exchange(query_grad.reshape(HEADS, SHARD, DH), SETS))
    key_out, value_out = unpack_two(
        exchange_groups(total.astype(bf16).reshape(HEADS, SHARD, 2 * DH))
    )
    return (query_out[None], key_out[None], value_out[None])


def solution(mesh):
    spec = P("blk", "seq", None)
    return jax.shard_map(
        per_device,
        mesh=mesh,
        in_specs=(spec,) * 6 + (P("blk", "seq"),),
        out_specs=(spec,) * 3,
        check_vma=False,
    )
```

time: 550 us -> 230 us (0.42)
  blocking collectives: 124 us -> 0 us
  matrix products: 71 us -> 0 us
  loops' own time: 64.8 us -> 0 us
  waiting for transfers between devices: 168 us -> 112 us
  Pallas kernels: 0 us -> 54.8 us
  local copies, waits for them, and re-layouts: 39.9 us -> 4.12 us
  other arithmetic: 33.2 us -> 3.68 us
  starting transfers between devices: 30.2 us -> 53.9 us
  between operations: 15.1 us -> 0.99 us
    reduce_scatter x2 -> x0, waiting for transfers between devices: 158 us -> none  [the longest x1 130 us: per_device(): lax.psum_scatter(key_parts.reshape(all_rows, -1).astype(jnp.bfloat16), 'b...]
    all_to_all x5 -> x0, blocking collectives: 91 us -> none  [the longest x1 23.6 us: per_device(): lax.all_to_all(student_key[0], 'seq', split_axis=1, concat_axis=0, tiled=...]
    dot_general x53 -> x0, matrix products: 71 us -> none  [the longest x19 30.1 us: softmax_step(): jnp.einsum('hqk,khd->hqd', weights.astype(jnp.bfloat16), split_heads(valu...]
    another operation x35 -> x0, loops' own time: 64.8 us -> none  [the longest x2 32.9 us: over_blocks(): lax.scan(over_advance, state, (stacked, jnp.arange(block_count, dtype=jnp...]
    ppermute x0 -> x24, waiting for transfers between devices: none -> 61 us  [the longest x12 57.9 us: chip_shift(): lax.ppermute(x, 'blk', [(i, (i // 2 + by) % 4 * 2 + i % 2) for i in range...]
    pallas_call x0 -> x6, Pallas kernels: none -> 54.8 us  [the longest x1 28.2 us: student(): pl.pallas_call(student_kernel, out_shape=[jax.ShapeDtypeStruct((ROWS, DH)...]
    all_to_all x4, waiting for transfers between devices: 9.21 us -> 51.3 us  [the longest x2 45.3 us: exchange_groups(): lax.all_to_all(packed, 'seq', split_axis=0, concat_axis=0, tiled=True)]
    all_gather x2 -> x0, blocking collectives: 33.1 us -> none  [the longest x1 20 us: per_device(): group_frames = lax.all_gather(frame_index[0], 'seq', axis=0, tiled=True)]
  transfers between devices with their start and end apart: 10 -> 28, of which waited for: 3 -> 10; matrix products, arithmetic and copies ran while one was open for 7% -> 2% of each run, Pallas kernels for 0% -> 9%
where the time goes in v1:
time: 230 us
  waiting for transfers between devices  112 us (49%)
  Pallas kernels  54.8 us (24%)
  starting transfers between devices  53.9 us (23%)
  local copies, waits for them, and re-layouts  4.12 us (2%)
  other arithmetic  3.68 us (2%)
    ppermute x12, waiting for transfers between devices, chip_shift(): lax.ppermute(x, 'blk', [(i, (i // 2 + by) % 4 * 2 + i % 2) for i in range...  57.9 us
    all_to_all x2, waiting for transfers between devices, exchange_groups(): lax.all_to_all(packed, 'seq', split_axis=0, concat_axis=0, tiled=True)  45.3 us
    pallas_call x1, Pallas kernels, student(): pl.pallas_call(student_kernel, out_shape=[jax.ShapeDtypeStruct((ROWS, DH)...  28.2 us
    ppermute x12, starting transfers between devices, chip_shift(): lax.ppermute(x, 'blk', [(i, (i // 2 + by) % 4 * 2 + i % 2) for i in range...  18.7 us
    pallas_call x1, Pallas kernels, teacher(): pl.pallas_call(teacher_kernel, out_shape=jax.ShapeDtypeStruct((DH, ROWS),...  18.6 us
    all_to_all x2, starting transfers between devices, exchange_groups(): lax.all_to_all(packed, 'seq', split_axis=0, concat_axis=0, tiled=True)  16.3 us
    all_to_all x2, starting transfers between devices, exchange(): lax.all_to_all(packed, AXES, split_axis=0, concat_axis=0, tiled=True, axi...  16.1 us
    all_to_all x2, waiting for transfers between devices, exchange(): lax.all_to_all(packed, AXES, split_axis=0, concat_axis=0, tiled=True, axi...  5.92 us
  transfers between devices with their start and end apart: 28, of which 10 were waited for; matrix products, arithmetic and copies ran while one was open for 2% of the time, Pallas kernels for 9%

profile of v1, /device:TPU:32, one launch (start us, length us, event | category | flops | bytes accessed | tf_op | source)
XLA Modules:
  0.0 229.7 jit_solution(4390749951171971484)
XLA Ops:
  0.6 2.4 %shard_map.112 = bf16[32,64,256]{2,1,0:T(8,128)(2,1)} custom-call(bf16[32,4096]{1,0:T(8,128)(2,1)} %bitcast.55, bf16[32,4096]{1,0:T(8,128)(2,1)} %bitcast.56, bf16[32,4096]{1,0:T(8,128)(2,1)} %bitcast.57, bf16[32,4096]{1,0:T(8,128)(2,1)} %bitcast.58), custom_call_target="tpu_custom_call" | custom-call | tf_op jit(solution)/shard_map/pallas_call | solution.py:66
  3.0 11.4 %all-to-all-start = ((bf16[32,64,256]{2,1,0:T(8,128)(2,1)}), bf16[32,64,256]{2,1,0:T(8,128)(2,1)S(1)}, u32[]{:S(2)}, u32[]{:S(2)}) async-start(bf16[32,64,256]{2,1,0:T(8,128)(2,1)} %shard_map.112), calls=%async_computation | async-start | bytes 2097152 | tf_op jit(solution)/shard_map/all_to_all | solution.py:358
  14.5 28.4 %all-to-all-done = bf16[32,64,256]{2,1,0:T(8,128)(2,1)S(1)} async-done(((bf16[32,64,256]{2,1,0:T(8,128)(2,1)}), bf16[32,64,256]{2,1,0:T(8,128)(2,1)S(1)}, u32[]{:S(2)}, u32[]{:S(2)}) %all-to-all-start) | async-done | bytes 1048608 | tf_op jit(solution)/shard_map/all_to_all | solution.py:358
  43.5 2.0 shard_map.113
  45.5 6.3 %all-to-all-start.1 = ((bf16[32,48,256]{2,1,0:T(8,128)(2,1)}), bf16[32,48,256]{2,1,0:T(8,128)(2,1)S(1)}, u32[]{:S(2)}, u32[]{:S(2)}) async-start(bf16[32,48,256]{2,1,0:T(8,128)(2,1)} %shard_map.113), calls=%async_computation.1 | async-start | bytes 1572864 | tf_op jit(solution)/shard_map/all_to_all | solution.py:352
  52.2 3.0 %collective-permute-start.8 = (bf16[1024,256]{1,0:T(8,128)(2,1)S(1)}, bf16[1024,256]{1,0:T(8,128)(2,1)}, u32[]{:S(2)}, u32[]{:S(2)}) collective-permute-start(bf16[1024,256]{1,0:T(8,128)(2,1)S(1)} %bitcast.43), channel_id=1, source_target_pairs={{0,6},{1,7},{2,0},{3,1},{4,2},{5,3},{6,4},{7,5},{8,14},{9,15},{10,... | collective-permute-start | bytes 1572872 | tf_op jit(solution)/shard_map/ppermute | solution.py:362
  55.6 31.0 %collective-permute-done.10.rest_4_ = bf16[1024,256]{1,0:T(8,128)(2,1)S(1)} collective-permute-done((bf16[1024,256]{1,0:T(8,128)(2,1)S(1)}, bf16[1024,256]{1,0:T(8,128)(2,1)S(1)}, u32[]{:S(2)}, u32[]{:S(2)}) %collective-permute-start.10) | collective-permute-done | bytes 524320 | tf_op jit(solution)/shard_map/ppermute | solution.py:362
  87.2 0.7 concatenate.17.meta_ref
  88.1 3.8 %collective-permute-start.5 = (bf16[1024,256]{1,0:T(8,128)(2,1)S(1)}, bf16[1024,256]{1,0:T(8,128)(2,1)}, u32[]{:S(2)}, u32[]{:S(2)}) collective-permute-start(bf16[1024,256]{1,0:T(8,128)(2,1)S(1)} %bitcast.48), channel_id=1, source_target_pairs={{0,2},{1,3},{2,4},{3,5},{4,6},{5,7},{6,0},{7,1},{8,10},{9,11},{10,... | collective-permute-start | bytes 1572872 | tf_op jit(solution)/shard_map/ppermute | solution.py:362
  92.1 18.6 %shard_map.114.target_ref = bf16[128,1024]{1,0:T(8,128)(2,1)} custom-call(s32[24]{0:T(128)} %concatenate.17.meta_ref, bf16[32,48,256]{2,1,0:T(8,128)(2,1)} %copy-done.3, bf16[1024,256]{1,0:T(8,128)(2,1)} %bitcast.46, bf16[1024,256]{1,0:T(8,128)(2,1)} %collective-permute-done.7.rest_1_, bf16[1024,256]{1,0:T(8,128)(2,1)} %collective-permute-done.8.rest_2_, ...), custom_call_target="tpu_custom_call" | custom-call | flops 16000000000 | bytes 6291456 | tf_op jit(solution)/shard_map/pallas_call | solution.py:173
  110.7 4.3 %collective-permute-done.5.rest_4_ = bf16[1024,256]{1,0:T(8,128)(2,1)} collective-permute-done((bf16[1024,256]{1,0:T(8,128)(2,1)S(1)}, bf16[1024,256]{1,0:T(8,128)(2,1)}, u32[]{:S(2)}, u32[]{:S(2)}) %collective-permute-start.5) | collective-permute-done | bytes 524320 | tf_op jit(solution)/shard_map/ppermute | solution.py:362
  116.4 5.2 %collective-permute-done.1 = f32[8,128]{0,1:T(8,128)S(1)} collective-permute-done((f32[8,128]{0,1:T(8,128)S(1)}, f32[8,128]{0,1:T(8,128)S(1)}, u32[]{:S(2)}, u32[]{:S(2)}) %collective-permute-start.1) | collective-permute-done | bytes 4128 | tf_op jit(solution)/shard_map/ppermute | solution.py:362
  122.2 5.2 %collective-permute-done.2 = f32[8,128]{0,1:T(8,128)S(1)} collective-permute-done((f32[8,128]{0,1:T(8,128)S(1)}, f32[8,128]{0,1:T(8,128)S(1)}, u32[]{:S(2)}, u32[]{:S(2)}) %collective-permute-start.2) | collective-permute-done | bytes 4128 | tf_op jit(solution)/shard_map/ppermute | solution.py:362
  127.5 0.6 concatenate.16.meta_ref
  128.2 0.7 copy-done.9
  129.4 28.2 %shard_map.115 = (bf16[1024,128]{1,0:T(8,128)(2,1)}, bf16[1024,256]{1,0:T(8,128)(2,1)}, bf16[1024,256]{1,0:T(8,128)(2,1)}, bf16[2,1024,256]{2,1,0:T(8,128)(2,1)}...) custom-call(s32[24]{0:T(128)} %concatenate.16.meta_ref, ...), custom_call_target="tpu_custom_call" | custom-call | flops 25999998976 | bytes 10485760 | tf_op jit(solution)/shard_map/pallas_call | solution.py:326
  158.3 3.0 %collective-permute-done.19 = bf16[1024,256]{1,0:T(8,128)(2,1)S(1)} collective-permute-done((bf16[1024,256]{1,0:T(8,128)(2,1)}, bf16[1024,256]{1,0:T(8,128)(2,1)S(1)}, u32[]{:S(2)}, u32[]{:S(2)}) %collective-permute-start.19) | collective-permute-done | bytes 524320 | tf_op jit(solution)/shard_map/ppermute | solution.py:366
  161.3 1.2 add_convert_fusion.1
  162.5 2.4 %collective-permute-start.20 = (bf16[512,256]{1,0:T(8,128)(2,1)S(1)}, bf16[512,256]{1,0:T(8,128)(2,1)S(1)}, u32[]{:S(2)}, u32[]{:S(2)}) collective-permute-start(bf16[512,256]{1,0:T(8,128)(2,1)S(1)} %get-tuple-element.43), channel_id=1, source_target_pairs={{0,2},{1,3},{2,4},{3,5},{4,6},{5,7},{6,0},{7,1},{8,10},{9,11},{10,... | collective-permute-start | bytes 786440 | tf_op jit(solution)/shard_map/ppermute | solution.py:362
  164.9 4.9 %collective-permute-start.22 = (bf16[512,256]{1,0:T(8,128)(2,1)S(1)}, bf16[512,256]{1,0:T(8,128)(2,1)S(1)}, u32[]{:S(2)}, u32[]{:S(2)}) collective-permute-start(bf16[512,256]{1,0:T(8,128)(2,1)S(1)} %get-tuple-element.44), channel_id=1, source_target_pairs={{0,6},{1,7},{2,0},{3,1},{4,2},{5,3},{6,4},{7,5},{8,14},{9,15},{10,... | collective-permute-start | bytes 786440 | tf_op jit(solution)/shard_map/ppermute | solution.py:362
  170.1 6.2 %collective-permute-done.20 = bf16[512,256]{1,0:T(8,128)(2,1)S(1)} collective-permute-done((bf16[512,256]{1,0:T(8,128)(2,1)S(1)}, bf16[512,256]{1,0:T(8,128)(2,1)S(1)}, u32[]{:S(2)}, u32[]{:S(2)}) %collective-permute-start.20) | collective-permute-done | bytes 262176 | tf_op jit(solution)/shard_map/ppermute | solution.py:362
  176.5 3.3 %collective-permute-start.23 = (bf16[1024,256]{1,0:T(8,128)(2,1)S(1)}, bf16[1024,256]{1,0:T(8,128)(2,1)S(1)}, u32[]{:S(2)}, u32[]{:S(2)}) collective-permute-start(bf16[1024,256]{1,0:T(8,128)(2,1)S(1)} %pad_maximum_fusion.1), channel_id=1, source_target_pairs={{0,6},{1,7},{2,0},{3,1},{4,2},{5,3},{6,4},{7,5},{8,14},{9,15},{10,... | collective-permute-start | bytes 1572872 | tf_op jit(solution)/shard_map/ppermute | solution.py:362
  179.8 0.8 pad_maximum_fusion
  180.6 9.8 %all-to-all-start.2 = ((bf16[32,32,128]{2,1,0:T(8,128)(2,1)}), bf16[32,32,128]{2,1,0:T(8,128)(2,1)S(1)}, u32[]{:S(2)}, u32[]{:S(2)}) async-start(bf16[32,32,128]{2,1,0:T(8,128)(2,1)} %bitcast.20), calls=%async_computation.2 | async-start | bytes 524288 | tf_op jit(solution)/shard_map/all_to_all | solution.py:352
  190.4 6.0 %collective-permute-done.21 = bf16[1024,256]{1,0:T(8,128)(2,1)S(1)} collective-permute-done((bf16[1024,256]{1,0:T(8,128)(2,1)}, bf16[1024,256]{1,0:T(8,128)(2,1)S(1)}, u32[]{:S(2)}, u32[]{:S(2)}) %collective-permute-start.21) | collective-permute-done | bytes 524320 | tf_op jit(solution)/shard_map/ppermute | solution.py:362
  196.4 1.1 add_convert_fusion
  197.5 5.9 %all-to-all-done.2.in_ref = bf16[32,32,128]{2,1,0:T(8,128)(2,1)S(1)} async-done(((bf16[32,32,128]{2,1,0:T(8,128)(2,1)}), bf16[32,32,128]{2,1,0:T(8,128)(2,1)S(1)}, u32[]{:S(2)}, u32[]{:S(2)}) %all-to-all-start.2) | async-done | bytes 262176 | tf_op jit(solution)/shard_map/all_to_all | solution.py:352
  203.4 5.0 %all-to-all-start.3 = ((bf16[32,32,256]{2,1,0:T(8,128)(2,1)}), bf16[32,32,256]{2,1,0:T(8,128)(2,1)S(1)}, u32[]{:S(2)}, u32[]{:S(2)}) async-start(bf16[32,32,256]{2,1,0:T(8,128)(2,1)} %bitcast.26), calls=%async_computation.3 | async-start | bytes 1048576 | tf_op jit(solution)/shard_map/all_to_all | solution.py:358
  208.4 1.7 shard_map.116
  210.1 16.9 %all-to-all-done.3.in_ref = bf16[32,32,256]{2,1,0:T(8,128)(2,1)S(1)} async-done(((bf16[32,32,256]{2,1,0:T(8,128)(2,1)}), bf16[32,32,256]{2,1,0:T(8,128)(2,1)S(1)}, u32[]{:S(2)}, u32[]{:S(2)}) %all-to-all-start.3) | async-done | bytes 524320 | tf_op jit(solution)/shard_map/all_to_all | solution.py:358
  227.0 0.8 copy-done
  227.8 1.9 shard_map.117
  (80 shorter events, 6.0 us)
Async XLA Ops:
  3.0 39.9 %all-to-all-start = ((bf16[32,64,256]{2,1,0:T(8,128)(2,1)}), bf16[32,64,256]{2,1,0:T(8,128)(2,1)S(1)}, u32[]{:S(2)}, u32[]{:S(2)}) async-start(bf16[32,64,256]{2,1,0:T(8,128)(2,1)} %shard_map.112), calls=%async_computation | async-start | bytes 2097152 | tf_op jit(solution)/shard_map/all_to_all | solution.py:358
  14.4 72.8 %copy-start.13 = (s32[2]{0:T(128)S(1)}, s32[2]{0:T(128)}, u32[]{:S(2)}) copy-start(s32[2]{0:T(128)} %constant.83.clone) | copy-start | bytes 28
  45.5 42.5 %all-to-all-start.1 = ((bf16[32,48,256]{2,1,0:T(8,128)(2,1)}), bf16[32,48,256]{2,1,0:T(8,128)(2,1)S(1)}, u32[]{:S(2)}, u32[]{:S(2)}) async-start(bf16[32,48,256]{2,1,0:T(8,128)(2,1)} %shard_map.113), calls=%async_computation.1 | async-start | bytes 1572864 | tf_op jit(solution)/shard_map/all_to_all | solution.py:352
  51.9 40.2 %copy-start.5 = (bf16[32,32,256]{2,1,0:T(8,128)(2,1)}, bf16[32,32,256]{2,1,0:T(8,128)(2,1)S(1)}, u32[]{:S(2)}) copy-start(bf16[32,32,256]{2,1,0:T(8,128)(2,1)S(1)} %slice.47) | copy-start | bytes 1572868
  51.9 34.6 %collective-permute-start.10 = (bf16[1024,256]{1,0:T(8,128)(2,1)S(1)}, bf16[1024,256]{1,0:T(8,128)(2,1)S(1)}, u32[]{:S(2)}, u32[]{:S(2)}) collective-permute-start(bf16[1024,256]{1,0:T(8,128)(2,1)S(1)} %bitcast.42), channel_id=1, source_target_pairs={{0,2},{1,3},{2,4},{3,5},{4,6},{5,7},{6,0},{7,1},{8,10},{9,11},{10,... | collective-permute-start | bytes 1572872 | tf_op jit(solution)/shard_map/ppermute | solution.py:362
  52.2 34.4 %collective-permute-start.8 = (bf16[1024,256]{1,0:T(8,128)(2,1)S(1)}, bf16[1024,256]{1,0:T(8,128)(2,1)}, u32[]{:S(2)}, u32[]{:S(2)}) collective-permute-start(bf16[1024,256]{1,0:T(8,128)(2,1)S(1)} %bitcast.43), channel_id=1, source_target_pairs={{0,6},{1,7},{2,0},{3,1},{4,2},{5,3},{6,4},{7,5},{8,14},{9,15},{10,... | collective-permute-start | bytes 1572872 | tf_op jit(solution)/shard_map/ppermute | solution.py:362
  55.2 31.8 %collective-permute-start.3 = (bf16[1024,256]{1,0:T(8,128)(2,1)S(1)}, bf16[1024,256]{1,0:T(8,128)(2,1)}, u32[]{:S(2)}, u32[]{:S(2)}) collective-permute-start(bf16[1024,256]{1,0:T(8,128)(2,1)S(1)} %bitcast.44), channel_id=1, source_target_pairs={{0,4},{1,5},{2,6},{3,7},{4,0},{5,1},{6,2},{7,3},{8,12},{9,13},{10,... | collective-permute-start | bytes 1572872 | tf_op jit(solution)/shard_map/ppermute | solution.py:362
  55.2 32.9 %collective-permute-start.7 = (bf16[1024,256]{1,0:T(8,128)(2,1)S(1)}, bf16[1024,256]{1,0:T(8,128)(2,1)}, u32[]{:S(2)}, u32[]{:S(2)}) collective-permute-start(bf16[1024,256]{1,0:T(8,128)(2,1)S(1)} %bitcast.45), channel_id=1, source_target_pairs={{0,1},{1,0},{2,3},{3,2},{4,5},{5,4},{6,7},{7,6},{8,9},{9,8},{10,11... | collective-permute-start | bytes 1572872 | tf_op jit(solution)/shard_map/ppermute | solution.py:366
  86.6 5.4 %collective-permute-start.11 = (bf16[1024,256]{1,0:T(8,128)(2,1)S(1)}, bf16[1024,256]{1,0:T(8,128)(2,1)}, u32[]{:S(2)}, u32[]{:S(2)}) collective-permute-start(bf16[1024,256]{1,0:T(8,128)(2,1)S(1)} %collective-permute-done.10.rest_4_), channel_id=1, source_target_pairs={{0,1},{1,0},{2,3},{3,2},{4,5},{5,4},{6,7},{7,6},{8,9},{9,8},{10,11... | collective-permute-start | bytes 1572872 | tf_op jit(solution)/shard_map/ppermute | solution.py:366
  86.6 5.3 %collective-permute-start.9 = (bf16[1024,256]{1,0:T(8,128)(2,1)}, bf16[1024,256]{1,0:T(8,128)(2,1)}, u32[]{:S(2)}, u32[]{:S(2)}) collective-permute-start(bf16[1024,256]{1,0:T(8,128)(2,1)} %collective-permute-done.8.rest_2_), channel_id=1, source_target_pairs={{0,1},{1,0},{2,3},{3,2},{4,5},{5,4},{6,7},{7,6},{8,9},{9,8},{10,11... | collective-permute-start | bytes 1572872 | tf_op jit(solution)/shard_map/ppermute | solution.py:366
  87.1 5.0 %collective-permute-start.12 = (bf16[1024,256]{1,0:T(8,128)(2,1)}, bf16[1024,256]{1,0:T(8,128)(2,1)}, u32[]{:S(2)}, u32[]{:S(2)}) collective-permute-start(bf16[1024,256]{1,0:T(8,128)(2,1)} %collective-permute-done.3.rest_6_), channel_id=1, source_target_pairs={{0,1},{1,0},{2,3},{3,2},{4,5},{5,4},{6,7},{7,6},{8,9},{9,8},{10,11... | collective-permute-start | bytes 1572872 | tf_op jit(solution)/shard_map/ppermute | solution.py:366
  87.9 27.1 %copy-start.6 = (bf16[32,32,256]{2,1,0:T(8,128)(2,1)}, bf16[32,32,256]{2,1,0:T(8,128)(2,1)S(1)}, u32[]{:S(2)}) copy-start(bf16[32,32,256]{2,1,0:T(8,128)(2,1)S(1)} %slice.36) | copy-start | bytes 1572868
  87.9 22.8 %collective-permute-start.6 = (bf16[1024,256]{1,0:T(8,128)(2,1)S(1)}, bf16[1024,256]{1,0:T(8,128)(2,1)S(1)}, u32[]{:S(2)}, u32[]{:S(2)}) collective-permute-start(bf16[1024,256]{1,0:T(8,128)(2,1)S(1)} %bitcast.47), channel_id=1, source_target_pairs={{0,4},{1,5},{2,6},{3,7},{4,0},{5,1},{6,2},{7,3},{8,12},{9,13},{10,... | collective-permute-start | bytes 1572872 | tf_op jit(solution)/shard_map/ppermute | solution.py:362
  88.1 26.9 %collective-permute-start.5 = (bf16[1024,256]{1,0:T(8,128)(2,1)S(1)}, bf16[1024,256]{1,0:T(8,128)(2,1)}, u32[]{:S(2)}, u32[]{:S(2)}) collective-permute-start(bf16[1024,256]{1,0:T(8,128)(2,1)S(1)} %bitcast.48), channel_id=1, source_target_pairs={{0,2},{1,3},{2,4},{3,5},{4,6},{5,7},{6,0},{7,1},{8,10},{9,11},{10,... | collective-permute-start | bytes 1572872 | tf_op jit(solution)/shard_map/ppermute | solution.py:362
  91.9 23.1 %collective-permute-start.4 = (bf16[1024,256]{1,0:T(8,128)(2,1)S(1)}, bf16[1024,256]{1,0:T(8,128)(2,1)}, u32[]{:S(2)}, u32[]{:S(2)}) collective-permute-start(bf16[1024,256]{1,0:T(8,128)(2,1)S(1)} %bitcast.49), channel_id=1, source_target_pairs={{0,6},{1,7},{2,0},{3,1},{4,2},{5,3},{6,4},{7,5},{8,14},{9,15},{10,... | collective-permute-start | bytes 1572872 | tf_op jit(solution)/shard_map/ppermute | solution.py:362
  92.0 24.1 %collective-permute-start = (f32[8,128]{0,1:T(8,128)S(1)}, f32[8,128]{0,1:T(8,128)S(1)}, u32[]{:S(2)}, u32[]{:S(2)}) collective-permute-start(f32[8,128]{0,1:T(8,128)S(1)} %broadcast_in_dim.20), channel_id=1, source_target_pairs={{0,1},{1,0},{2,3},{3,2},{4,5},{5,4},{6,7},{7,6},{8,9},{9,8},{10,11... | collective-permute-start | bytes 12296 | tf_op jit(solution)/shard_map/ppermute | solution.py:366
  115.0 13.1 %collective-permute-start.13 = (bf16[1024,256]{1,0:T(8,128)(2,1)S(1)}, bf16[1024,256]{1,0:T(8,128)(2,1)S(1)}, u32[]{:S(2)}, u32[]{:S(2)}) collective-permute-start(bf16[1024,256]{1,0:T(8,128)(2,1)S(1)} %bitcast.50), channel_id=1, source_target_pairs={{0,1},{1,0},{2,3},{3,2},{4,5},{5,4},{6,7},{7,6},{8,9},{9,8},{10,11... | collective-permute-start | bytes 1572872 | tf_op jit(solution)/shard_map/ppermute | solution.py:366
  115.0 13.1 %collective-permute-start.14 = (bf16[1024,256]{1,0:T(8,128)(2,1)}, bf16[1024,256]{1,0:T(8,128)(2,1)S(1)}, u32[]{:S(2)}, u32[]{:S(2)}) collective-permute-start(bf16[1024,256]{1,0:T(8,128)(2,1)} %collective-permute-done.4.rest_2_), channel_id=1, source_target_pairs={{0,1},{1,0},{2,3},{3,2},{4,5},{5,4},{6,7},{7,6},{8,9},{9,8},{10,11... | collective-permute-start | bytes 1572872 | tf_op jit(solution)/shard_map/ppermute | solution.py:366
  115.5 12.6 %collective-permute-start.15 = (bf16[1024,256]{1,0:T(8,128)(2,1)}, bf16[1024,256]{1,0:T(8,128)(2,1)S(1)}, u32[]{:S(2)}, u32[]{:S(2)}) collective-permute-start(bf16[1024,256]{1,0:T(8,128)(2,1)} %collective-permute-done.5.rest_4_), channel_id=1, source_target_pairs={{0,1},{1,0},{2,3},{3,2},{4,5},{5,4},{6,7},{7,6},{8,9},{9,8},{10,11... | collective-permute-start | bytes 1572872 | tf_op jit(solution)/shard_map/ppermute | solution.py:366
  115.6 12.5 %collective-permute-start.16 = (bf16[1024,256]{1,0:T(8,128)(2,1)S(1)}, bf16[1024,256]{1,0:T(8,128)(2,1)}, u32[]{:S(2)}, u32[]{:S(2)}) collective-permute-start(bf16[1024,256]{1,0:T(8,128)(2,1)S(1)} %collective-permute-done.6.rest_6_), channel_id=1, source_target_pairs={{0,1},{1,0},{2,3},{3,2},{4,5},{5,4},{6,7},{7,6},{8,9},{9,8},{10,11... | collective-permute-start | bytes 1572872 | tf_op jit(solution)/shard_map/ppermute | solution.py:366
  116.0 5.6 %collective-permute-start.1 = (f32[8,128]{0,1:T(8,128)S(1)}, f32[8,128]{0,1:T(8,128)S(1)}, u32[]{:S(2)}, u32[]{:S(2)}) collective-permute-start(f32[8,128]{0,1:T(8,128)S(1)} %broadcast_add_fusion), channel_id=1, source_target_pairs={{0,2},{1,3},{2,4},{3,5},{4,6},{5,7},{6,0},{7,1},{8,10},{9,11},{10,... | collective-permute-start | bytes 12296 | tf_op jit(solution)/shard_map/ppermute | solution.py:362
  121.6 5.9 %collective-permute-start.2 = (f32[8,128]{0,1:T(8,128)S(1)}, f32[8,128]{0,1:T(8,128)S(1)}, u32[]{:S(2)}, u32[]{:S(2)}) collective-permute-start(f32[8,128]{0,1:T(8,128)S(1)} %fusion.9), channel_id=1, source_target_pairs={{0,4},{1,5},{2,6},{3,7},{4,0},{5,1},{6,2},{7,3},{8,12},{9,13},{10,... | collective-permute-start | bytes 12296 | tf_op jit(solution)/shard_map/ppermute | solution.py:362
  157.6 12.2 %collective-permute-start.18 = (bf16[2,1024,256]{2,1,0:T(8,128)(2,1)}, bf16[2,1024,256]{2,1,0:T(8,128)(2,1)S(1)}, u32[]{:S(2)}, u32[]{:S(2)}) collective-permute-start(bf16[2,1024,256]{2,1,0:T(8,128)(2,1)} %get-tuple-element.32), channel_id=1, source_target_pairs={{0,1},{1,0},{2,3},{3,2},{4,5},{5,4},{6,7},{7,6},{8,9},{9,8},{10,11... | collective-permute-start | bytes 3145736 | tf_op jit(solution)/shard_map/ppermute | solution.py:366
  157.7 3.6 %collective-permute-start.19 = (bf16[1024,256]{1,0:T(8,128)(2,1)}, bf16[1024,256]{1,0:T(8,128)(2,1)S(1)}, u32[]{:S(2)}, u32[]{:S(2)}) collective-permute-start(bf16[1024,256]{1,0:T(8,128)(2,1)} %get-tuple-element.34), channel_id=1, source_target_pairs={{0,1},{1,0},{2,3},{3,2},{4,5},{5,4},{6,7},{7,6},{8,9},{9,8},{10,11... | collective-permute-start | bytes 1572872 | tf_op jit(solution)/shard_map/ppermute | solution.py:366
  158.2 32.3 %collective-permute-start.17 = (bf16[1024,256]{1,0:T(8,128)(2,1)}, bf16[1024,256]{1,0:T(8,128)(2,1)S(1)}, u32[]{:S(2)}, u32[]{:S(2)}) collective-permute-start(bf16[1024,256]{1,0:T(8,128)(2,1)} %get-tuple-element.30), channel_id=1, source_target_pairs={{0,1},{1,0},{2,3},{3,2},{4,5},{5,4},{6,7},{7,6},{8,9},{9,8},{10,11... | collective-permute-start | bytes 1572872 | tf_op jit(solution)/shard_map/ppermute | solution.py:366
  162.5 13.8 %collective-permute-start.20 = (bf16[512,256]{1,0:T(8,128)(2,1)S(1)}, bf16[512,256]{1,0:T(8,128)(2,1)S(1)}, u32[]{:S(2)}, u32[]{:S(2)}) collective-permute-start(bf16[512,256]{1,0:T(8,128)(2,1)S(1)} %get-tuple-element.43), channel_id=1, source_target_pairs={{0,2},{1,3},{2,4},{3,5},{4,6},{5,7},{6,0},{7,1},{8,10},{9,11},{10,... | collective-permute-start | bytes 786440 | tf_op jit(solution)/shard_map/ppermute | solution.py:362
  164.9 11.4 %collective-permute-start.22 = (bf16[512,256]{1,0:T(8,128)(2,1)S(1)}, bf16[512,256]{1,0:T(8,128)(2,1)S(1)}, u32[]{:S(2)}, u32[]{:S(2)}) collective-permute-start(bf16[512,256]{1,0:T(8,128)(2,1)S(1)} %get-tuple-element.44), channel_id=1, source_target_pairs={{0,6},{1,7},{2,0},{3,1},{4,2},{5,3},{6,4},{7,5},{8,14},{9,15},{10,... | collective-permute-start | bytes 786440 | tf_op jit(solution)/shard_map/ppermute | solution.py:362
  176.3 20.2 %copy-start.4 = (bf16[1024,256]{1,0:T(8,128)(2,1)S(1)}, bf16[1024,256]{1,0:T(8,128)(2,1)}, u32[]{:S(2)}) copy-start(bf16[1024,256]{1,0:T(8,128)(2,1)} %get-tuple-element.29) | copy-start | bytes 1572868
  176.5 14.0 %collective-permute-start.23 = (bf16[1024,256]{1,0:T(8,128)(2,1)S(1)}, bf16[1024,256]{1,0:T(8,128)(2,1)S(1)}, u32[]{:S(2)}, u32[]{:S(2)}) collective-permute-start(bf16[1024,256]{1,0:T(8,128)(2,1)S(1)} %pad_maximum_fusion.1), channel_id=1, source_target_pairs={{0,6},{1,7},{2,0},{3,1},{4,2},{5,3},{6,4},{7,5},{8,14},{9,15},{10,... | collective-permute-start | bytes 1572872 | tf_op jit(solution)/shard_map/ppermute | solution.py:362
  180.6 15.8 %collective-permute-start.21 = (bf16[1024,256]{1,0:T(8,128)(2,1)}, bf16[1024,256]{1,0:T(8,128)(2,1)S(1)}, u32[]{:S(2)}, u32[]{:S(2)}) collective-permute-start(bf16[1024,256]{1,0:T(8,128)(2,1)} %pad_maximum_fusion), channel_id=1, source_target_pairs={{0,2},{1,3},{2,4},{3,5},{4,6},{5,7},{6,0},{7,1},{8,10},{9,11},{10,... | collective-permute-start | bytes 1572872 | tf_op jit(solution)/shard_map/ppermute | solution.py:362
  180.6 22.8 %all-to-all-start.2 = ((bf16[32,32,128]{2,1,0:T(8,128)(2,1)}), bf16[32,32,128]{2,1,0:T(8,128)(2,1)S(1)}, u32[]{:S(2)}, u32[]{:S(2)}) async-start(bf16[32,32,128]{2,1,0:T(8,128)(2,1)} %bitcast.20), calls=%async_computation.2 | async-start | bytes 524288 | tf_op jit(solution)/shard_map/all_to_all | solution.py:352
  203.4 23.6 %all-to-all-start.3 = ((bf16[32,32,256]{2,1,0:T(8,128)(2,1)}), bf16[32,32,256]{2,1,0:T(8,128)(2,1)S(1)}, u32[]{:S(2)}, u32[]{:S(2)}) async-start(bf16[32,32,256]{2,1,0:T(8,128)(2,1)} %bitcast.26), calls=%async_computation.3 | async-start | bytes 1048576 | tf_op jit(solution)/shard_map/all_to_all | solution.py:358
  (10 other events, 61.8 us)
